TPU v7x, 32 devices: a whole 2x2x4 slice. The times are simulated.
32 devices in a mesh: samp: 8 (over y, x, core), head: 4 (over z).
Axes of the slice: x: 2, y: 2, z: 4, core: 2. Of those that a mesh axis runs over, the one named last changes fastest.
Arguments:
- input_tokens: bfloat16 [16, 512, 768], P('samp'), may hold values from -6 to 6
- output_cotangent: bfloat16 [16, 512, 768], P('samp'), may hold values from -15 to 15
- query_weight: bfloat16 [768, 768], P(None, 'head'), may hold values from -0.21875 to 0.21875
- key_weight: bfloat16 [768, 768], P(None, 'head'), may hold values from -0.21875 to 0.21875
- value_weight: bfloat16 [768, 768], P(None, 'head'), may hold values from -0.21875 to 0.21875
- output_weight: bfloat16 [768, 768], P('head'), may hold values from -0.21875 to 0.21875
- pair_bias: bfloat16 [16, 512, 512], P('head'), may hold values from -6 to 240
- valid_len: int32 [1], replicated, may hold values from 256 to 512
- pair_in: bfloat16 [512, 512, 128], P('head', 'samp'), may hold values from -6 to 6
- w_bias: bfloat16 [128, 16], replicated, may hold values from -6 to 6
- t_gate: bfloat16 [2, 128, 256], replicated, may hold values from -0.5 to 0.5
- t_up: bfloat16 [2, 128, 256], replicated, may hold values from -0.5 to 0.5
- t_down: bfloat16 [2, 256, 128], replicated, may hold values from -0.375 to 0.375
Outputs:
- d_tokens: bfloat16 [16, 512, 768], P('samp', None, 'head')
- d_pair: bfloat16 [512, 512, 128], P('head', 'samp')
- d_trans_gate: float32 [2, 128, 256], replicated
- d_trans_up: float32 [2, 128, 256], replicated
- d_trans_down: float32 [2, 256, 128], replicated
All inputs are finite; a program needn't handle non-finite values.
Results may differ from a plain program's by a relative error of at most 0.02.
Values may be sent and summed in bfloat16 or wider, within the bound.
A program may use at most 128 MiB of HBM per device.

v0:
```python
import functools
import math

import jax
import jax.numpy as jnp
from jax import lax
from jax.experimental import pallas as pl
from jax.experimental.pallas import tpu as pltpu
from jax.sharding import PartitionSpec as P

HD = 48
LANES = 128

EPS_NORM = 1e-05
MASKED = -1e30
VMEM_LIMIT = 56 * 1024 * 1024
MESH = pl.DeviceIdType.MESH


def dot(lhs, rhs, lhs_dim=1, rhs_dim=0):
    return lax.dot_general(
        lhs, rhs, (((lhs_dim,), (rhs_dim,)), ((), ())), preferred_element_type=jnp.float32
    )


def attention_kernel(
    rows,
    valid_ref,
    tokens_ref,
    cotangent_ref,
    wq_ref,
    wk_ref,
    wv_ref,
    wo_ref,
    spread_ref,
    bias_ref,
    terms_ref,
    part_ref,
    wide_in,
    wide_out,
    projected,
    attn_grad,
    joined,
    key_sum,
    value_sum,
    bias_sum,
):
    step = pl.program_id(0)
    heads, tokens, _ = bias_ref.shape
    width = heads * LANES
    scale = 1.0 / math.sqrt(HD)

    @pl.when(step == 0)
    def _():
        spread = spread_ref[...]
        for which, ref in enumerate((wq_ref, wk_ref, wv_ref)):
            wide_in[:, which * width : (which + 1) * width] = dot(ref[...], spread).astype(
                jnp.bfloat16
            )
        wide_out[...] = dot(spread, wo_ref[...], 0, 0).astype(jnp.bfloat16)
        bias_sum[...] = jnp.zeros_like(bias_sum)

    projected[...] = dot(tokens_ref[0], wide_in[...]).astype(jnp.bfloat16)
    attn_grad[...] = dot(cotangent_ref[0], wide_out[...], 1, 1).astype(jnp.bfloat16)
    kept = lax.broadcasted_iota(jnp.int32, (1, tokens), 1) < valid_ref[0]

    for head in range(heads):
        q_cols = slice(head * LANES, (head + 1) * LANES)
        k_cols = slice(width + head * LANES, width + (head + 1) * LANES)
        v_cols = slice(2 * width + head * LANES, 2 * width + (head + 1) * LANES)
        keys = projected[:, k_cols]
        values = projected[:, v_cols]
        for block in range(tokens // rows):
            span = slice(block * rows, (block + 1) * rows)
            query = projected[span, q_cols]
            grad_out = attn_grad[span, q_cols]
            scores = dot(query, keys, 1, 1) * scale + bias_ref[head, span].astype(jnp.float32)
            scores = jnp.where(kept, scores, MASKED)
            exp_scores = jnp.exp(scores - jnp.max(scores, axis=-1, keepdims=True))
            probs = exp_scores * (1.0 / jnp.sum(exp_scores, axis=-1, keepdims=True))
            grad_probs = dot(grad_out, values, 1, 1)
            delta = jnp.sum(probs * grad_probs, axis=-1, keepdims=True)
            grad_scores = probs * (grad_probs - delta)
            scores_low = grad_scores.astype(jnp.bfloat16)
            bias_sum[head, span] += grad_scores
            joined[span, q_cols] = (dot(scores_low, keys) * scale).astype(jnp.bfloat16)
            key_term = dot(scores_low, query, 0, 0)
            value_term = dot(probs.astype(jnp.bfloat16), grad_out, 0, 0)
            if block == 0:
                key_sum[...] = key_term
                value_sum[...] = value_term
            else:
                key_sum[...] += key_term
                value_sum[...] += value_term
        joined[:, k_cols] = (key_sum[...] * scale).astype(jnp.bfloat16)
        joined[:, v_cols] = value_sum[...].astype(jnp.bfloat16)

    terms_ref[0] = dot(joined[...], wide_in[...], 1, 1).astype(jnp.bfloat16)

    @pl.when(step == pl.num_programs(0) - 1)
    def _():
        part_ref[...] = bias_sum[...].astype(jnp.bfloat16)


def attention(tokens_in, cotangent, wq, wk, wv, wo, bias, valid_len):
    samples, tokens, features = tokens_in.shape
    heads = bias.shape[0]
    width = heads * LANES
    source = lax.broadcasted_iota(jnp.int32, (heads * HD, width), 0)
    place = lax.broadcasted_iota(jnp.int32, (heads * HD, width), 1)
    spread = (place == (source // HD) * LANES + source % HD).astype(jnp.bfloat16)
    vmem = pl.BlockSpec(memory_space=pltpu.VMEM)
    per_sample = pl.BlockSpec((1, tokens, features), lambda s: (s, 0, 0))
    whole_bias = pl.BlockSpec(bias.shape, lambda s: (0, 0, 0))
    return pl.pallas_call(
        functools.partial(attention_kernel, min(128, tokens)),
        grid=(samples,),
        in_specs=[pl.BlockSpec(memory_space=pltpu.SMEM), per_sample, per_sample]
        + [vmem] * 6,
        out_specs=[per_sample, whole_bias],
        out_shape=[
            jax.ShapeDtypeStruct(tokens_in.shape, jnp.bfloat16),
            jax.ShapeDtypeStruct(bias.shape, jnp.bfloat16),
        ],
        scratch_shapes=[
            pltpu.VMEM((features, 3 * width), jnp.bfloat16),
            pltpu.VMEM((width, features), jnp.bfloat16),
            pltpu.VMEM((tokens, 3 * width), jnp.bfloat16),
            pltpu.VMEM((tokens, width), jnp.bfloat16),
            pltpu.VMEM((tokens, 3 * width), jnp.bfloat16),
            pltpu.VMEM((tokens, LANES), jnp.float32),
            pltpu.VMEM((tokens, LANES), jnp.float32),
            pltpu.VMEM(bias.shape, jnp.float32),
        ],
        compiler_params=pltpu.CompilerParams(vmem_limit_bytes=VMEM_LIMIT),
        name="attention",
    )(valid_len, tokens_in, cotangent, wq, wk, wv, wo, spread, bias)


def pair_kernel(
    pair_ref, bias_ref, wb_ref, tg_ref, tu_ref, td_ref, dpair_ref, sums_ref, totals
):
    step = pl.program_id(0)
    layers, channels, _ = tg_ref.shape

    @pl.when(step == 0)
    def _():
        totals[...] = jnp.zeros_like(totals)

    field = pair_ref[...].astype(jnp.float32)
    saved = []
    for layer in range(layers):
        centred = field - jnp.mean(field, axis=-1, keepdims=True)
        variance = jnp.mean(centred * centred, axis=-1, keepdims=True)
        inv_std = lax.rsqrt(variance + EPS_NORM)
        normed = centred * inv_std
        low = normed.astype(jnp.bfloat16)
        gate = dot(low, tg_ref[layer])
        up = dot(low, tu_ref[layer])
        sig = 0.5 * jnp.tanh(0.5 * gate) + 0.5
        act = gate * sig
        hidden = (act * up).astype(jnp.bfloat16)
        saved.append((normed, low, inv_std, gate, up, sig, act, hidden))
        if layer + 1 < layers:
            field = field + dot(hidden, td_ref[layer])
    grad = dot(bias_ref[...], wb_ref[...], 0, 0)
    for layer in reversed(range(layers)):
        normed, low, inv_std, gate, up, sig, act, hidden = saved[layer]
        grad_low = grad.astype(jnp.bfloat16)
        grad_hidden = dot(grad_low, td_ref[layer], 1, 1)
        grad_gate = (grad_hidden * up * (sig + act * (1.0 - sig))).astype(jnp.bfloat16)
        grad_up = (grad_hidden * act).astype(jnp.bfloat16)
        for which, term in enumerate(
            (dot(low, grad_gate, 0, 0), dot(low, grad_up, 0, 0), dot(grad_low, hidden, 0, 0))
        ):
            first = (which * layers + layer) * channels
            totals[first : first + channels] += term
        grad_normed = dot(grad_gate, tg_ref[layer], 1, 1) + dot(grad_up, tu_ref[layer], 1, 1)
        grad = grad + inv_std * (
            grad_normed
            - jnp.mean(grad_normed, axis=-1, keepdims=True)
            - normed * jnp.mean(grad_normed * normed, axis=-1, keepdims=True)
        )
    dpair_ref[...] = grad.astype(jnp.bfloat16)

    @pl.when(step == pl.num_programs(0) - 1)
    def _():
        sums_ref[...] = totals[...].astype(jnp.bfloat16)


def pair_transitions(pair, bias_grad, w_bias, t_gate, t_up, t_down):
    pairs, channels = pair.shape
    heads = bias_grad.shape[0]
    layers, _, hidden = t_gate.shape
    tile = math.gcd(pairs, 1024)
    vmem = pl.BlockSpec(memory_space=pltpu.VMEM)
    sums = (3 * layers * channels, hidden)
    return pl.pallas_call(
        pair_kernel,
        grid=(pairs // tile,),
        in_specs=[
            pl.BlockSpec((tile, channels), lambda i: (i, 0)),
            pl.BlockSpec((heads, tile), lambda i: (0, i)),
        ]
        + [vmem] * 4,
        out_specs=[
            pl.BlockSpec((tile, channels), lambda i: (i, 0)),
            pl.BlockSpec(sums, lambda i: (0, 0)),
        ],
        out_shape=[
            jax.ShapeDtypeStruct(pair.shape, jnp.bfloat16),
            jax.ShapeDtypeStruct(sums, jnp.bfloat16),
        ],
        scratch_shapes=[pltpu.VMEM(sums, jnp.float32)],
        compiler_params=pltpu.CompilerParams(vmem_limit_bytes=VMEM_LIMIT),
        name="pair_transitions",
    )(pair, bias_grad, w_bias.T, t_gate, t_up, t_down)


def sum_kernel(
    groups,
    heads,
    divisor,
    part_ref,
    total_ref,
    landed,
    crossed,
    gathered,
    send_a,
    recv_a,
    send_b,
    recv_b,
    send_c,
    recv_c,
):
    samp, head = lax.axis_index("samp"), lax.axis_index("head")
    rows = gathered.shape[1]
    barrier = pltpu.get_barrier_semaphore()
    for k in range(1, groups):
        other = (lax.rem(samp + k, groups), head)
        pl.semaphore_signal(barrier, inc=1, device_id=other, device_id_type=MESH)
    for k in range(1, heads):
        other = (samp, lax.rem(head + k, heads))
        pl.semaphore_signal(barrier, inc=1, device_id=other, device_id_type=MESH)
    pl.semaphore_wait(barrier, groups - 1 + heads - 1)

    def piece(index):
        return pl.ds(pl.multiple_of(index * rows, 16), rows)

    scatter = []
    for k in range(1, groups):
        other = lax.rem(samp + k, groups)
        copy = pltpu.make_async_remote_copy(
            src_ref=part_ref.at[piece(other)],
            dst_ref=landed.at[k],
            send_sem=send_a.at[k],
            recv_sem=recv_a.at[k],
            device_id=(other, head),
            device_id_type=MESH,
        )
        copy.start()
        scatter.append(copy)
    running = part_ref[piece(samp)].astype(jnp.float32)
    for k, copy in enumerate(scatter):
        copy.wait_recv()
        running = running + landed[k + 1].astype(jnp.float32)
    crossed[head] = running.astype(jnp.bfloat16)
    cross = []
    for k in range(1, heads):
        copy = pltpu.make_async_remote_copy(
            src_ref=crossed.at[head],
            dst_ref=crossed.at[head],
            send_sem=send_b.at[k],
            recv_sem=recv_b.at[k],
            device_id=(samp, lax.rem(head + k, heads)),
            device_id_type=MESH,
        )
        copy.start()
        cross.append(copy)
    for copy in cross:
        copy.wait_recv()
    running = crossed[0].astype(jnp.float32)
    for k in range(1, heads):
        running = running + crossed[k].astype(jnp.float32)
    gathered[samp] = running.astype(jnp.bfloat16)
    gather = []
    for k in range(1, groups):
        copy = pltpu.make_async_remote_copy(
            src_ref=gathered.at[samp],
            dst_ref=gathered.at[samp],
            send_sem=send_c.at[k],
            recv_sem=recv_c.at[k],
            device_id=(lax.rem(samp + k, groups), head),
            device_id_type=MESH,
        )
        copy.start()
        gather.append(copy)
    for copy in gather:
        copy.wait_recv()
    for k in range(groups):
        total_ref[k] = gathered[k].astype(jnp.float32) / divisor
    for copy in scatter + cross + gather:
        copy.wait_send()


def sum_everywhere(part, groups, heads, divisor):
    size, width = part.shape
    rows = size // groups
    vmem = pl.BlockSpec(memory_space=pltpu.VMEM)
    return pl.pallas_call(
        functools.partial(sum_kernel, groups, heads, divisor),
        in_specs=[vmem],
        out_specs=vmem,
        out_shape=jax.ShapeDtypeStruct((groups, rows, width), jnp.float32),
        scratch_shapes=[
            pltpu.VMEM((groups, rows, width), jnp.bfloat16),
            pltpu.VMEM((heads, rows, width), jnp.bfloat16),
            pltpu.VMEM((groups, rows, width), jnp.bfloat16),
        ]
        + [pltpu.SemaphoreType.DMA((n,)) for n in (groups, groups, heads, heads, groups, groups)],
        compiler_params=pltpu.CompilerParams(
            collective_id=0, has_side_effects=True, vmem_limit_bytes=VMEM_LIMIT
        ),
        name="sum_everywhere",
    )(part).reshape(size, width)


def per_device(
    groups,
    head_groups,
    input_tokens,
    output_cotangent,
    query_weight,
    key_weight,
    value_weight,
    output_weight,
    pair_bias,
    valid_len,
    pair_in,
    w_bias,
    t_gate,
    t_up,
    t_down,
):
    tokens = input_tokens.shape[1]
    token_terms, bias_parts = attention(
        input_tokens,
        output_cotangent,
        query_weight,
        key_weight,
        value_weight,
        output_weight,
        pair_bias,
        valid_len,
    )
    d_tokens = lax.psum_scatter(token_terms, "head", scatter_dimension=2, tiled=True)
    summed = lax.psum_scatter(bias_parts, "samp", scatter_dimension=2, tiled=True)
    owned_grad = lax.all_to_all(summed, "head", split_axis=1, concat_axis=0, tiled=True)
    pair_rows, pair_cols, channels = pair_in.shape
    d_pair, sums = pair_transitions(
        pair_in.reshape(pair_rows * pair_cols, channels),
        owned_grad.reshape(owned_grad.shape[0], pair_rows * pair_cols),
        w_bias,
        t_gate,
        t_up,
        t_down,
    )
    totals = sum_everywhere(sums, groups, head_groups, tokens)
    layers, _, hidden = t_gate.shape
    totals = totals.reshape(3, layers, channels, hidden)
    return (
        d_tokens,
        d_pair.reshape(pair_in.shape),
        totals[0],
        totals[1],
        totals[2].transpose(0, 2, 1),
    )


def solution(mesh):
    placed = (
        P("samp", None, None),
        P("samp", None, None),
        P(None, "head"),
        P(None, "head"),
        P(None, "head"),
        P("head", None),
        P("head", None, None),
        P(),
        P("head", "samp", None),
        P(),
        P(),
        P(),
        P(),
    )
    return jax.shard_map(
        functools.partial(per_device, mesh.shape["samp"], mesh.shape["head"]),
        mesh=mesh,
        in_specs=placed,
        out_specs=(P("samp", None, "head"), P("head", "samp", None), P(), P(), P()),
        check_vma=False,
    )
```

profile of v0, /device:TPU:0, one launch (start us, length us, event | category | flops | bytes accessed | tf_op | source)
XLA Modules:
  0.0 209.9 jit_solution(8611072301098817957)
XLA Ops:
  7.9 1.9 copy.30.wq_ref
  9.8 1.9 copy.31.wk_ref
  11.7 1.9 copy.32.wv_ref
  13.5 0.9 fusion.spread_ref
  14.4 30.6 %attention.1 = (bf16[2,512,768]{2,1,0:T(8,128)(2,1)}, bf16[4,512,512]{2,1,0:T(8,128)(2,1)}) custom-call(s32[1]{0:T(128)S(6)} %copy.44.valid_ref, bf16[2,512,768]{2,1,0:T(8,128)(2,1)} %tokens_ref.1, bf16[2,512,768]{2,1,0:T(8,128)(2,1)} %cotangent_ref.1, bf16[768,192]{1,0:T(8,128)(2,1)} %copy.30.wq_ref, bf16[768,192]{1,0:T(8,128)(2,1)} %copy.31.wk_ref, ...), custom_call_target="tpu_custom_call" | custom-call | tf_op jit(solution)/shard_map/attention/pallas_call | solution.py:115
  45.0 4.5 %copy.34 = bf16[4,512,512]{1,0,2:T(4,128)(2,1)} copy(bf16[4,512,512]{2,1,0:T(8,128)(2,1)} %get-tuple-element.10) | data formatting | bytes 4194304 | tf_op jit(solution)/shard_map/attention/pallas_call | solution.py:115
  49.8 1.2 copy-done
  50.9 3.0 %copy.33 = bf16[2,512,768]{1,0,2:T(2,128)(2,1)} copy(bf16[2,512,768]{2,1,0:T(8,128)(2,1)S(1)} %copy-done) | data formatting | bytes 3145728 | tf_op jit(solution)/shard_map/attention/pallas_call | solution.py:115
  54.0 0.6 dynamic-slice.2
  55.2 58.6 %all-reduce.7.cloned.1.call-done = bf16[4,512,512]{1,0,2:T(4,128)(2,1)} async-done(((bf16[4,512,512]{1,0,2:T(4,128)(2,1)}), bf16[4,512,512]{1,0,2:T(4,128)(2,1)}) %all-reduce.7.cloned.1.call-update) | async-done | bytes 2097168
  113.8 1.0 constant_dynamic-slice_fusion
  114.9 0.4 copy.35
  115.2 1.1 reshape.25
  116.3 4.6 %all-to-all-start = ((bf16[4,2,16384]{2,1,0:T(2,128)(2,1)}), bf16[4,2,16384]{2,1,0:T(2,128)(2,1)S(1)}, u32[]{:S(2)}, u32[]{:S(2)}) async-start(bf16[4,2,16384]{2,1,0:T(2,128)(2,1)} %reshape.25), calls=%async_computation | async-start | bytes 524288 | tf_op jit(solution)/shard_map/all_to_all | solution.py:358
  121.0 0.6 dynamic-slice
  122.2 13.9 %all-to-all-done = bf16[4,2,16384]{2,1,0:T(2,128)(2,1)S(1)} async-done(((bf16[4,2,16384]{2,1,0:T(2,128)(2,1)}), bf16[4,2,16384]{2,1,0:T(2,128)(2,1)S(1)}, u32[]{:S(2)}, u32[]{:S(2)}) %all-to-all-start) | async-done | bytes 262176 | tf_op jit(solution)/shard_map/all_to_all | solution.py:358
  136.1 0.3 reshape.26
  136.6 1.2 reshape.21.bias_ref
  137.7 36.9 %pair_transitions.1 = (bf16[8192,128]{1,0:T(8,128)(2,1)}, bf16[768,256]{1,0:T(8,128)(2,1)}) custom-call(bf16[8192,128]{1,0:T(8,128)(2,1)} %bitcast.23, bf16[16,8192]{1,0:T(8,128)(2,1)} %reshape.21.bias_ref, bf16[16,128]{1,0:T(8,128)(2,1)} %bitcast.27, bf16[2,128,256]{2,1,0:T(8,128)(2,1)} %tg_ref.1, bf16[2,128,256]{2,1,0:T(8,128)(2,1)} %tu_ref.1, ...), custom_call_target="tpu_custom_call" | custom-call | tf_op jit(solution)/shard_map/pair_transitions/pallas_call | solution.py:198
  174.6 23.5 %sum_everywhere.1 = f32[8,96,256]{2,1,0:T(8,128)} custom-call(bf16[768,256]{1,0:T(8,128)(2,1)} %get-tuple-element.12.part_ref), custom_call_target="tpu_custom_call" | custom-call | tf_op jit(solution)/shard_map/sum_everywhere/pallas_call | solution.py:310
  198.1 2.0 fusion.3
  200.1 0.8 copy.39
  201.0 1.3 constant_dynamic-slice_fusion.1
  202.2 0.8 copy.38
  (14 shorter events, 0.4 us)
Async XLA Ops:
  7.2 106.7 %all-reduce.7.cloned.1.call-start = ((), (), s32[]{:S(2)}) async-start(), calls=%async_computation.2 | async-start | bytes 4194304
  49.5 1.4 copy-start
  49.5 151.4 %all-reduce.5.cloned.1.call-start = ((), (), s32[]{:S(2)}) async-start(), calls=%async_computation.1 | async-start | bytes 3145728
  50.9 3.1 %copy-start.2 = (u32[32]{0:T(128)S(1)}, u32[32]{0:T(128)}, u32[]{:S(2)}) copy-start(u32[32]{0:T(128)} %constant.30) | copy-start | bytes 388
  53.9 67.0 %copy-start.1 = (u32[32]{0:T(128)S(1)}, u32[32]{0:T(128)}, u32[]{:S(2)}) copy-start(u32[32]{0:T(128)} %constant.26) | copy-start | bytes 388
  116.3 19.8 %all-to-all-start = ((bf16[4,2,16384]{2,1,0:T(2,128)(2,1)}), bf16[4,2,16384]{2,1,0:T(2,128)(2,1)S(1)}, u32[]{:S(2)}, u32[]{:S(2)}) async-start(bf16[4,2,16384]{2,1,0:T(2,128)(2,1)} %reshape.25), calls=%async_computation | async-start | bytes 524288 | tf_op jit(solution)/shard_map/all_to_all | solution.py:358
Sparse Core Ops, SparseCore 0:
  49.7 64.1 all-reduce.6
  116.2 76.8 all-reduce.4
where the time goes:
time: 211 us; the launch traced here: 210 us
  Pallas kernels  91 us (43%)
  waiting for transfers between devices  72.5 us (34%)
  local copies, waits for them, and re-layouts  24.5 us (12%)
  between operations  16.1 us (8%)
  starting transfers between devices  4.88 us (2%)
    unnamed x4, waiting for transfers between devices  58.6 us
    pallas_call x1, Pallas kernels, pair_transitions(): pl.pallas_call(pair_kernel, grid=(pairs // tile,), in_specs=[pl.BlockSpec...  36.9 us
    pallas_call x1, Pallas kernels, attention(): pl.pallas_call(functools.partial(attention_kernel, min(128, tokens)), gri...  30.6 us
    pallas_call x1, Pallas kernels, sum_everywhere(): pl.pallas_call(functools.partial(sum_kernel, groups, heads, divisor), in_...  23.5 us
    all_to_all x1, waiting for transfers between devices, per_device(): lax.all_to_all(summed, 'head', split_axis=1, concat_axis=0, tiled=True)  13.9 us
    unnamed x17, local copies, waits for them, and re-layouts  13.3 us
    pallas_call x2, local copies, waits for them, and re-layouts, attention(): pl.pallas_call(functools.partial(attention_kernel, min(128, tokens)), gri...  7.52 us
    all_to_all x1, starting transfers between devices, per_device(): lax.all_to_all(summed, 'head', split_axis=1, concat_axis=0, tiled=True)  4.62 us
  transfers between devices with their start and end apart: 3, of which 2 were waited for; matrix products, arithmetic and copies ran while one was open for 5% of the time, Pallas kernels for 29%

commit v1 on v0

--- a/solution.py
+++ b/solution.py
@@ -95,11 +95,12 @@
         joined[:, k_cols] = (key_sum[...] * scale).astype(jnp.bfloat16)
         joined[:, v_cols] = value_sum[...].astype(jnp.bfloat16)
 
-    terms_ref[0] = dot(joined[...], wide_in[...], 1, 1).astype(jnp.bfloat16)
+    terms_ref[0] = dot(wide_in[...], joined[...], 1, 1).astype(jnp.bfloat16)
 
     @pl.when(step == pl.num_programs(0) - 1)
     def _():
-        part_ref[...] = bias_sum[...].astype(jnp.bfloat16)
+        for head in range(heads):
+            part_ref[head] = bias_sum[head].T.astype(jnp.bfloat16)
 
 
 def attention(tokens_in, cotangent, wq, wk, wv, wo, bias, valid_len):
@@ -117,9 +118,9 @@
         grid=(samples,),
         in_specs=[pl.BlockSpec(memory_space=pltpu.SMEM), per_sample, per_sample]
         + [vmem] * 6,
-        out_specs=[per_sample, whole_bias],
+        out_specs=[pl.BlockSpec((1, features, tokens), lambda s: (s, 0, 0)), whole_bias],
         out_shape=[
-            jax.ShapeDtypeStruct(tokens_in.shape, jnp.bfloat16),
+            jax.ShapeDtypeStruct((samples, features, tokens), jnp.bfloat16),
             jax.ShapeDtypeStruct(bias.shape, jnp.bfloat16),
         ],
         scratch_shapes=[
@@ -138,16 +139,26 @@
 
 
 def pair_kernel(
-    pair_ref, bias_ref, wb_ref, tg_ref, tu_ref, td_ref, dpair_ref, sums_ref, totals
+    pair_ref, bias_ref, wb_ref, tg_ref, tu_ref, td_ref, dpair_ref, sums_ref, totals, grad_top
 ):
-    step = pl.program_id(0)
+    outer, inner = pl.program_id(0), pl.program_id(1)
     layers, channels, _ = tg_ref.shape
-
-    @pl.when(step == 0)
+    part_rows, columns, _ = pair_ref.shape
+    rows = bias_ref.shape[2]
+    tile = part_rows * columns
+
+    @pl.when((outer == 0) & (inner == 0))
     def _():
         totals[...] = jnp.zeros_like(totals)
 
-    field = pair_ref[...].astype(jnp.float32)
+    @pl.when(inner == 0)
+    def _():
+        for column in range(columns):
+            grad_top[pl.ds(column, rows, stride=columns), :] = dot(
+                bias_ref[:, column, :].astype(jnp.bfloat16), wb_ref[...], 0, 0
+            )
+
+    field = pair_ref[...].reshape(tile, channels).astype(jnp.float32)
     saved = []
     for layer in range(layers):
         centred = field - jnp.mean(field, axis=-1, keepdims=True)
@@ -163,7 +174,7 @@
         saved.append((normed, low, inv_std, gate, up, sig, act, hidden))
         if layer + 1 < layers:
             field = field + dot(hidden, td_ref[layer])
-    grad = dot(bias_ref[...], wb_ref[...], 0, 0)
+    grad = grad_top[pl.ds(pl.multiple_of(inner * tile, 16), tile), :]
     for layer in reversed(range(layers)):
         normed, low, inv_std, gate, up, sig, act, hidden = saved[layer]
         grad_low = grad.astype(jnp.bfloat16)
@@ -181,37 +192,41 @@
             - jnp.mean(grad_normed, axis=-1, keepdims=True)
             - normed * jnp.mean(grad_normed * normed, axis=-1, keepdims=True)
         )
-    dpair_ref[...] = grad.astype(jnp.bfloat16)
-
-    @pl.when(step == pl.num_programs(0) - 1)
+    dpair_ref[...] = grad.astype(jnp.bfloat16).reshape(dpair_ref.shape)
+
+    @pl.when((outer == pl.num_programs(0) - 1) & (inner == pl.num_programs(1) - 1))
     def _():
         sums_ref[...] = totals[...].astype(jnp.bfloat16)
 
 
 def pair_transitions(pair, bias_grad, w_bias, t_gate, t_up, t_down):
-    pairs, channels = pair.shape
+    rows, columns, channels = pair.shape
     heads = bias_grad.shape[0]
     layers, _, hidden = t_gate.shape
-    tile = math.gcd(pairs, 1024)
+    part_rows, part_columns = math.gcd(rows, 64), math.gcd(columns, 16)
     vmem = pl.BlockSpec(memory_space=pltpu.VMEM)
+    pair_spec = pl.BlockSpec((part_rows, part_columns, channels), lambda j, i: (i, j, 0))
     sums = (3 * layers * channels, hidden)
     return pl.pallas_call(
         pair_kernel,
-        grid=(pairs // tile,),
+        grid=(columns // part_columns, rows // part_rows),
         in_specs=[
-            pl.BlockSpec((tile, channels), lambda i: (i, 0)),
-            pl.BlockSpec((heads, tile), lambda i: (0, i)),
+            pair_spec,
+            pl.BlockSpec((heads, part_columns, rows), lambda j, i: (0, j, 0)),
         ]
         + [vmem] * 4,
         out_specs=[
-            pl.BlockSpec((tile, channels), lambda i: (i, 0)),
-            pl.BlockSpec(sums, lambda i: (0, 0)),
+            pair_spec,
+            pl.BlockSpec(sums, lambda j, i: (0, 0)),
         ],
         out_shape=[
             jax.ShapeDtypeStruct(pair.shape, jnp.bfloat16),
             jax.ShapeDtypeStruct(sums, jnp.bfloat16),
         ],
-        scratch_shapes=[pltpu.VMEM(sums, jnp.float32)],
+        scratch_shapes=[
+            pltpu.VMEM(sums, jnp.float32),
+            pltpu.VMEM((rows * part_columns, channels), jnp.float32),
+        ],
         compiler_params=pltpu.CompilerParams(vmem_limit_bytes=VMEM_LIMIT),
         name="pair_transitions",
     )(pair, bias_grad, w_bias.T, t_gate, t_up, t_down)
@@ -323,6 +338,132 @@
         ),
         name="sum_everywhere",
     )(part).reshape(size, width)
+
+
+def exchange_kernel(
+    groups,
+    head_groups,
+    part_ref,
+    owned_ref,
+    from_pair,
+    paired,
+    from_chip,
+    reduced,
+    by_head,
+    send_a,
+    recv_a,
+    send_b,
+    recv_b,
+    send_c,
+    recv_c,
+):
+    samp, head = lax.axis_index("samp"), lax.axis_index("head")
+    heads, columns, _ = from_pair.shape[1:]
+    rows = by_head.shape[3]
+    chips = groups // 2
+    chip, core = samp // 2, lax.rem(samp, 2)
+    partner = chip * 2 + 1 - core
+    barrier = pltpu.get_barrier_semaphore()
+    pl.semaphore_signal(barrier, inc=1, device_id=(partner, head), device_id_type=MESH)
+    for k in range(1, chips):
+        other = lax.rem(chip + k, chips) * 2 + core
+        pl.semaphore_signal(barrier, inc=1, device_id=(other, head), device_id_type=MESH)
+    for k in range(1, head_groups):
+        other = lax.rem(head + k, head_groups)
+        pl.semaphore_signal(barrier, inc=1, device_id=(samp, other), device_id_type=MESH)
+    pl.semaphore_wait(barrier, 1 + chips - 1 + head_groups - 1)
+
+    def piece(owner):
+        return pl.ds(pl.multiple_of(owner * columns, 16), columns)
+
+    order = list(range(1, chips)) + [0]
+    pair_copies = []
+    for k in order:
+        target = lax.rem(chip + k, chips)
+        copy = pltpu.make_async_remote_copy(
+            src_ref=part_ref.at[:, piece(target * 2 + 1 - core)],
+            dst_ref=from_pair.at[k],
+            send_sem=send_a.at[k],
+            recv_sem=recv_a.at[k],
+            device_id=(partner, head),
+            device_id_type=MESH,
+        )
+        copy.start()
+        pair_copies.append(copy)
+    chip_copies = []
+    running = None
+    for k, pair_copy in zip(order, pair_copies):
+        target = lax.rem(chip + k, chips)
+        pair_copy.wait_recv()
+        both = part_ref[:, piece(target * 2 + core)].astype(jnp.float32) + from_pair[k].astype(
+            jnp.float32
+        )
+        if k == 0:
+            running = both
+            continue
+        paired[k] = both.astype(jnp.bfloat16)
+        copy = pltpu.make_async_remote_copy(
+            src_ref=paired.at[k],
+            dst_ref=from_chip.at[k],
+            send_sem=send_b.at[k],
+            recv_sem=recv_b.at[k],
+            device_id=(target * 2 + core, head),
+            device_id_type=MESH,
+        )
+        copy.start()
+        chip_copies.append(copy)
+    for k, copy in enumerate(chip_copies):
+        copy.wait_recv()
+        running = running + from_chip[k + 1].astype(jnp.float32)
+    low = running.astype(jnp.bfloat16)
+    for k in range(head_groups):
+        reduced[k] = low[:, :, k * rows : (k + 1) * rows]
+    by_head[head] = reduced[head]
+    head_copies = []
+    for k in range(1, head_groups):
+        other = lax.rem(head + k, head_groups)
+        copy = pltpu.make_async_remote_copy(
+            src_ref=reduced.at[other],
+            dst_ref=by_head.at[head],
+            send_sem=send_c.at[k],
+            recv_sem=recv_c.at[k],
+            device_id=(samp, other),
+            device_id_type=MESH,
+        )
+        copy.start()
+        head_copies.append(copy)
+    for copy in head_copies:
+        copy.wait_recv()
+    for k in range(head_groups):
+        owned_ref[k * heads : (k + 1) * heads] = by_head[k].astype(jnp.float32)
+    for copy in pair_copies + chip_copies + head_copies:
+        copy.wait_send()
+
+
+def exchange_bias(parts, groups, head_groups):
+    heads, tokens, _ = parts.shape
+    columns, rows = tokens // groups, tokens // head_groups
+    if groups % 2 or rows % LANES or columns % 16:
+        summed = lax.psum_scatter(parts, "samp", scatter_dimension=1, tiled=True)
+        owned = lax.all_to_all(summed, "head", split_axis=2, concat_axis=0, tiled=True)
+        return owned.astype(jnp.float32)
+    chips = groups // 2
+    vmem = pl.BlockSpec(memory_space=pltpu.VMEM)
+    landing = pltpu.VMEM((chips, heads, columns, tokens), jnp.bfloat16)
+    crossing = pltpu.VMEM((head_groups, heads, columns, rows), jnp.bfloat16)
+    counts = (chips, chips, chips, chips, head_groups, head_groups)
+    return pl.pallas_call(
+        functools.partial(exchange_kernel, groups, head_groups),
+        in_specs=[vmem],
+        out_specs=vmem,
+        out_shape=jax.ShapeDtypeStruct((head_groups * heads, columns, rows), jnp.float32),
+        scratch_shapes=[landing, landing, landing, crossing, crossing]
+        + [pltpu.SemaphoreType.DMA((n,)) for n in counts],
+        compiler_params=pltpu.CompilerParams(
+            collective_id=1, has_side_effects=True, vmem_limit_bytes=VMEM_LIMIT
+        ),
+        name="exchange_bias",
+    )(parts)
 
 
 def per_device(
@@ -353,24 +494,16 @@
         pair_bias,
         valid_len,
     )
-    d_tokens = lax.psum_scatter(token_terms, "head", scatter_dimension=2, tiled=True)
-    summed = lax.psum_scatter(bias_parts, "samp", scatter_dimension=2, tiled=True)
-    owned_grad = lax.all_to_all(summed, "head", split_axis=1, concat_axis=0, tiled=True)
-    pair_rows, pair_cols, channels = pair_in.shape
-    d_pair, sums = pair_transitions(
-        pair_in.reshape(pair_rows * pair_cols, channels),
-        owned_grad.reshape(owned_grad.shape[0], pair_rows * pair_cols),
-        w_bias,
-        t_gate,
-        t_up,
-        t_down,
-    )
+    d_tokens = lax.psum_scatter(token_terms, "head", scatter_dimension=1, tiled=True)
+    d_tokens = d_tokens.transpose(0, 2, 1)
+    owned_grad = exchange_bias(bias_parts, groups, head_groups)
+    d_pair, sums = pair_transitions(pair_in, owned_grad, w_bias, t_gate, t_up, t_down)
     totals = sum_everywhere(sums, groups, head_groups, tokens)
     layers, _, hidden = t_gate.shape
-    totals = totals.reshape(3, layers, channels, hidden)
+    totals = totals.reshape(3, layers, pair_in.shape[2], hidden)
     return (
         d_tokens,
-        d_pair.reshape(pair_in.shape),
+        d_pair,
         totals[0],
         totals[1],
         totals[2].transpose(0, 2, 1),

time: 211 us -> 150 us (0.71)
  waiting for transfers between devices: 72.5 us -> 0.02 us
  Pallas kernels: 91 us -> 125 us
  local copies, waits for them, and re-layouts: 24.5 us -> 8.5 us
  starting transfers between devices: 4.88 us -> 0.04 us
    unnamed x4 -> x1, waiting for transfers between devices: 58.6 us -> 0.02 us
    pallas_call x1 -> x2, Pallas kernels: 36.9 us -> 70 us  [the longest x1 36.7 us: pair_transitions(): pl.pallas_call(pair_kernel, grid=(columns // part_columns, rows // part_r...]
    all_to_all x1 -> x0, waiting for transfers between devices: 13.9 us -> none  [per_device(): lax.all_to_all(summed, 'head', split_axis=1, concat_axis=0, tiled=True)]
    pallas_call x2 -> x0, local copies, waits for them, and re-layouts: 7.52 us -> none  [attention(): pl.pallas_call(functools.partial(attention_kernel, min(128, tokens)), gri...]
    unnamed x17 -> x4, local copies, waits for them, and re-layouts: 13.3 us -> 6.52 us
    all_to_all x1 -> x0, starting transfers between devices: 4.62 us -> none  [per_device(): lax.all_to_all(summed, 'head', split_axis=1, concat_axis=0, tiled=True)]
    pallas_call x1, Pallas kernels: 23.5 us -> 25.9 us  [sum_everywhere(): pl.pallas_call(functools.partial(sum_kernel, groups, heads, divisor), in_...]
  transfers between devices with their start and end apart: 3 -> 1, of which waited for: 2 -> 0; matrix products, arithmetic and copies ran while one was open for 5% -> 2% of each run, Pallas kernels for 29% -> 64%
where the time goes in v1:
time: 150 us; the launch traced here: 149 us
  Pallas kernels  125 us (83%)
  between operations  14.7 us (10%)
  local copies, waits for them, and re-layouts  8.5 us (6%)
    pallas_call x1, Pallas kernels, pair_transitions(): pl.pallas_call(pair_kernel, grid=(columns // part_columns, rows // part_r...  36.7 us
    pallas_call x1, Pallas kernels, exchange_bias(): pl.pallas_call(functools.partial(exchange_kernel, groups, head_groups), i...  33.2 us
    pallas_call x1, Pallas kernels, attention(): pl.pallas_call(functools.partial(attention_kernel, min(128, tokens)), gri...  29.4 us
    pallas_call x1, Pallas kernels, sum_everywhere(): pl.pallas_call(functools.partial(sum_kernel, groups, heads, divisor), in_...  25.9 us
    unnamed x4, local copies, waits for them, and re-layouts  6.52 us
  transfers between devices with their start and end apart: 1, of which 0 were waited for; matrix products, arithmetic and copies ran while one was open for 2% of the time, Pallas kernels for 64%

profile of v1, /device:TPU:0, one launch (start us, length us, event | category | flops | bytes accessed | tf_op | source)
XLA Modules:
  0.0 149.4 jit_solution(8483628248037674038)
XLA Ops:
  7.2 0.0 reduce-scatter.2.cloned.1.call-start
  7.9 1.9 %copy.18.wq_ref = bf16[768,192]{1,0:T(8,128)(2,1)} copy(bf16[768,192]{0,1:T(8,128)(2,1)} %param.15) | data formatting | bytes 589824 | tf_op args[2]
  9.8 1.9 %copy.19.wk_ref = bf16[768,192]{1,0:T(8,128)(2,1)} copy(bf16[768,192]{0,1:T(8,128)(2,1)} %param.16) | data formatting | bytes 589824 | tf_op args[3]
  11.7 1.9 %copy.20.wv_ref = bf16[768,192]{1,0:T(8,128)(2,1)} copy(bf16[768,192]{0,1:T(8,128)(2,1)} %param.17) | data formatting | bytes 589824 | tf_op args[4]
  13.6 0.9 fusion.spread_ref
  14.5 29.4 %attention.1 = (bf16[2,768,512]{2,1,0:T(8,128)(2,1)}, bf16[4,512,512]{2,1,0:T(8,128)(2,1)}) custom-call(s32[1]{0:T(128)S(6)} %copy.23.valid_ref, bf16[2,512,768]{2,1,0:T(8,128)(2,1)} %tokens_ref.1, bf16[2,512,768]{2,1,0:T(8,128)(2,1)} %cotangent_ref.1, bf16[768,192]{1,0:T(8,128)(2,1)} %copy.18.wq_ref, bf16[768,192]{1,0:T(8,128)(2,1)} %copy.19.wk_ref, ...), custom_call_target="tpu_custom_call" | custom-call | tf_op jit(solution)/shard_map/attention/pallas_call | solution.py:116
  43.8 0.0 reduce-scatter.2.cloned.1.call-update
  43.9 33.2 %exchange_bias.1.bias_ref = f32[16,64,128]{2,1,0:T(8,128)} custom-call(bf16[4,512,512]{2,1,0:T(8,128)(2,1)} %get-tuple-element.10.part_ref), custom_call_target="tpu_custom_call" | custom-call | tf_op jit(solution)/shard_map/exchange_bias/pallas_call | solution.py:455
  77.1 36.7 %pair_transitions.1 = (bf16[128,64,128]{2,1,0:T(8,128)(2,1)}, bf16[768,256]{1,0:T(8,128)(2,1)}) custom-call(bf16[128,64,128]{2,1,0:T(8,128)(2,1)} %pair_ref.1, f32[16,64,128]{2,1,0:T(8,128)} %exchange_bias.1.bias_ref, bf16[16,128]{1,0:T(8,128)(2,1)} %bitcast.12, bf16[2,128,256]{2,1,0:T(8,128)(2,1)} %tg_ref.1, bf16[2,128,256]{2,1,0:T(8,128)(2,1)} %tu_ref.1, ...), custom_call_target="tpu_custom_call" | custom-call | tf_op jit(solution)/shard_map/pair_transitions/pallas_call | solution.py:210
  113.9 25.9 %sum_everywhere.1 = f32[8,96,256]{2,1,0:T(8,128)} custom-call(bf16[768,256]{1,0:T(8,128)(2,1)} %get-tuple-element.12.part_ref), custom_call_target="tpu_custom_call" | custom-call | tf_op jit(solution)/shard_map/sum_everywhere/pallas_call | solution.py:325
  139.7 2.0 %fusion.3 = (f32[1,2,128,256]{3,2,1,0:T(8,128)S(1)}, f32[2,128,256]{2,1,0:T(8,128)}, f32[2,128,256]{2,1,0:T(8,128)}) fusion(f32[3,2,128,256]{3,2,1,0:T(8,128)} %bitcast.10), kind=kLoop, calls=%fused_computation.12 | loop fusion | bytes 1572864 | tf_op jit(solution)/shard_map/slice | solution.py:509
  141.7 0.8 copy.22
  142.5 0.0 reduce-scatter.2.cloned.1.call-done
  (3 shorter events, 0.0 us)
Async XLA Ops:
  7.2 135.4 %reduce-scatter.2.cloned.1.call-start = ((), (), s32[]{:S(2)}) async-start(), calls=%async_computation.1 | async-start | bytes 1966080 | tf_op jit(solution)/shard_map/reduce_scatter | solution.py:497
Sparse Core Ops, SparseCore 0:
  44.0 42.1 reduce-scatter.1

commit v2 on v1

--- a/solution.py
+++ b/solution.py
@@ -54,7 +54,7 @@
     def _():
         spread = spread_ref[...]
         for which, ref in enumerate((wq_ref, wk_ref, wv_ref)):
-            wide_in[:, which * width : (which + 1) * width] = dot(ref[...], spread).astype(
+            wide_in[:, which * width : (which + 1) * width] = dot(ref[...], spread, 0, 0).astype(
                 jnp.bfloat16
             )
         wide_out[...] = dot(spread, wo_ref[...], 0, 0).astype(jnp.bfloat16)
@@ -135,7 +135,7 @@
         ],
         compiler_params=pltpu.CompilerParams(vmem_limit_bytes=VMEM_LIMIT),
         name="attention",
-    )(valid_len, tokens_in, cotangent, wq, wk, wv, wo, spread, bias)
+    )(valid_len, tokens_in, cotangent, wq.T, wk.T, wv.T, wo, spread, bias)
 
 
 def pair_kernel(
@@ -166,11 +166,11 @@
         inv_std = lax.rsqrt(variance + EPS_NORM)
         normed = centred * inv_std
         low = normed.astype(jnp.bfloat16)
-        gate = dot(low, tg_ref[layer])
-        up = dot(low, tu_ref[layer])
+        gate = dot(low, tg_ref[layer]).astype(jnp.bfloat16)
+        up = dot(low, tu_ref[layer]).astype(jnp.bfloat16)
         sig = 0.5 * jnp.tanh(0.5 * gate) + 0.5
         act = gate * sig
-        hidden = (act * up).astype(jnp.bfloat16)
+        hidden = act * up
         saved.append((normed, low, inv_std, gate, up, sig, act, hidden))
         if layer + 1 < layers:
             field = field + dot(hidden, td_ref[layer])
@@ -178,9 +178,9 @@
     for layer in reversed(range(layers)):
         normed, low, inv_std, gate, up, sig, act, hidden = saved[layer]
         grad_low = grad.astype(jnp.bfloat16)
-        grad_hidden = dot(grad_low, td_ref[layer], 1, 1)
-        grad_gate = (grad_hidden * up * (sig + act * (1.0 - sig))).astype(jnp.bfloat16)
-        grad_up = (grad_hidden * act).astype(jnp.bfloat16)
+        grad_hidden = dot(grad_low, td_ref[layer], 1, 1).astype(jnp.bfloat16)
+        grad_gate = grad_hidden * up * (sig + act * (1.0 - sig))
+        grad_up = grad_hidden * act
         for which, term in enumerate(
             (dot(low, grad_gate, 0, 0), dot(low, grad_up, 0, 0), dot(grad_low, hidden, 0, 0))
         ):

time: 150 us -> 143 us (0.953)
  local copies, waits for them, and re-layouts: 8.5 us -> 2.81 us
    unnamed x4 -> x1, local copies, waits for them, and re-layouts: 6.52 us -> 0.84 us
  transfers between devices with their start and end apart: 1 -> 1, of which waited for: 0 -> 0; matrix products, arithmetic and copies ran while one was open for 2% -> 2% of each run, Pallas kernels for 64% -> 67%
where the time goes in v2:
time: 143 us
  Pallas kernels  125 us (87%)
  between operations  14.7 us (10%)
  local copies, waits for them, and re-layouts  2.81 us (2%)
    pallas_call x1, Pallas kernels, pair_transitions(): pl.pallas_call(pair_kernel, grid=(columns // part_columns, rows // part_r...  36.3 us
    pallas_call x1, Pallas kernels, exchange_bias(): pl.pallas_call(functools.partial(exchange_kernel, groups, head_groups), i...  33.2 us
    pallas_call x1, Pallas kernels, attention(): pl.pallas_call(functools.partial(attention_kernel, min(128, tokens)), gri...  29.3 us
    pallas_call x1, Pallas kernels, sum_everywhere(): pl.pallas_call(functools.partial(sum_kernel, groups, heads, divisor), in_...  25.9 us
  transfers between devices with their start and end apart: 1, of which 0 were waited for; matrix products, arithmetic and copies ran while one was open for 2% of the time, Pallas kernels for 67%

profile of v2, /device:TPU:0, one launch (start us, length us, event | category | flops | bytes accessed | tf_op | source)
XLA Modules:
  0.0 143.2 jit_solution(1021064425277327990)
XLA Ops:
  7.2 0.0 reduce-scatter.2.cloned.1.call-start
  7.9 0.9 fusion.spread_ref
  8.8 29.3 %attention.1 = (bf16[2,768,512]{2,1,0:T(8,128)(2,1)}, bf16[4,512,512]{2,1,0:T(8,128)(2,1)}) custom-call(s32[1]{0:T(128)S(6)} %copy.20.valid_ref, bf16[2,512,768]{2,1,0:T(8,128)(2,1)} %tokens_ref.1, bf16[2,512,768]{2,1,0:T(8,128)(2,1)} %cotangent_ref.1, bf16[192,768]{1,0:T(8,128)(2,1)} %bitcast.14, bf16[192,768]{1,0:T(8,128)(2,1)} %bitcast.15, ...), custom_call_target="tpu_custom_call" | custom-call | tf_op jit(solution)/shard_map/attention/pallas_call | solution.py:116
  38.1 0.0 reduce-scatter.2.cloned.1.call-update
  38.2 33.2 %exchange_bias.1.bias_ref = f32[16,64,128]{2,1,0:T(8,128)} custom-call(bf16[4,512,512]{2,1,0:T(8,128)(2,1)} %get-tuple-element.10.part_ref), custom_call_target="tpu_custom_call" | custom-call | tf_op jit(solution)/shard_map/exchange_bias/pallas_call | solution.py:455
  71.4 36.3 %pair_transitions.1 = (bf16[128,64,128]{2,1,0:T(8,128)(2,1)}, bf16[768,256]{1,0:T(8,128)(2,1)}) custom-call(bf16[128,64,128]{2,1,0:T(8,128)(2,1)} %pair_ref.1, f32[16,64,128]{2,1,0:T(8,128)} %exchange_bias.1.bias_ref, bf16[16,128]{1,0:T(8,128)(2,1)} %bitcast.18, bf16[2,128,256]{2,1,0:T(8,128)(2,1)} %tg_ref.1, bf16[2,128,256]{2,1,0:T(8,128)(2,1)} %tu_ref.1, ...), custom_call_target="tpu_custom_call" | custom-call | tf_op jit(solution)/shard_map/pair_transitions/pallas_call | solution.py:210
  107.7 25.9 %sum_everywhere.1 = f32[8,96,256]{2,1,0:T(8,128)} custom-call(bf16[768,256]{1,0:T(8,128)(2,1)} %get-tuple-element.12.part_ref), custom_call_target="tpu_custom_call" | custom-call | tf_op jit(solution)/shard_map/sum_everywhere/pallas_call | solution.py:325
  133.6 2.0 %fusion.3 = (f32[1,2,128,256]{3,2,1,0:T(8,128)S(1)}, f32[2,128,256]{2,1,0:T(8,128)}, f32[2,128,256]{2,1,0:T(8,128)}) fusion(f32[3,2,128,256]{3,2,1,0:T(8,128)} %bitcast.13), kind=kLoop, calls=%fused_computation.12 | loop fusion | bytes 1572864 | tf_op jit(solution)/shard_map/slice | solution.py:509
  135.6 0.8 copy.19
  136.4 0.0 reduce-scatter.2.cloned.1.call-done
  (3 shorter events, 0.0 us)
Async XLA Ops:
  7.2 129.2 %reduce-scatter.2.cloned.1.call-start = ((), (), s32[]{:S(2)}) async-start(), calls=%async_computation.1 | async-start | bytes 1966080 | tf_op jit(solution)/shard_map/reduce_scatter | solution.py:497
Sparse Core Ops, SparseCore 0:
  38.3 42.1 reduce-scatter.1

commit v3 on v2

--- a/solution.py
+++ b/solution.py
@@ -114,7 +114,7 @@
     per_sample = pl.BlockSpec((1, tokens, features), lambda s: (s, 0, 0))
     whole_bias = pl.BlockSpec(bias.shape, lambda s: (0, 0, 0))
     return pl.pallas_call(
-        functools.partial(attention_kernel, min(128, tokens)),
+        functools.partial(attention_kernel, math.gcd(256, tokens)),
         grid=(samples,),
         in_specs=[pl.BlockSpec(memory_space=pltpu.SMEM), per_sample, per_sample]
         + [vmem] * 6,

time: 143 us -> 137 us (0.958)
  Pallas kernels: 125 us -> 118 us
    pallas_call x1, Pallas kernels: 29.3 us -> 22.9 us  [attention(): pl.pallas_call(functools.partial(attention_kernel, math.gcd(256, tokens))...]
  transfers between devices with their start and end apart: 1 -> 1, of which waited for: 0 -> 0; matrix products, arithmetic and copies ran while one was open for 2% -> 2% of each run, Pallas kernels for 67% -> 70%
where the time goes in v3:
time: 137 us
  Pallas kernels  118 us (86%)
  between operations  14.7 us (11%)
  local copies, waits for them, and re-layouts  2.81 us (2%)
    pallas_call x1, Pallas kernels, pair_transitions(): pl.pallas_call(pair_kernel, grid=(columns // part_columns, rows // part_r...  36.3 us
    pallas_call x1, Pallas kernels, exchange_bias(): pl.pallas_call(functools.partial(exchange_kernel, groups, head_groups), i...  33.2 us
    pallas_call x1, Pallas kernels, sum_everywhere(): pl.pallas_call(functools.partial(sum_kernel, groups, heads, divisor), in_...  25.9 us
    pallas_call x1, Pallas kernels, attention(): pl.pallas_call(functools.partial(attention_kernel, math.gcd(256, tokens))...  22.9 us
  transfers between devices with their start and end apart: 1, of which 0 were waited for; matrix products, arithmetic and copies ran while one was open for 2% of the time, Pallas kernels for 70%

profile of v3, /device:TPU:0, one launch (start us, length us, event | category | flops | bytes accessed | tf_op | source)
XLA Modules:
  0.0 136.8 jit_solution(18307887859895272708)
XLA Ops:
  7.2 0.0 reduce-scatter.2.cloned.1.call-start
  7.9 0.9 fusion.spread_ref
  8.8 22.9 %attention.1 = (bf16[2,768,512]{2,1,0:T(8,128)(2,1)}, bf16[4,512,512]{2,1,0:T(8,128)(2,1)}) custom-call(s32[1]{0:T(128)S(6)} %copy.20.valid_ref, bf16[2,512,768]{2,1,0:T(8,128)(2,1)} %tokens_ref.1, bf16[2,512,768]{2,1,0:T(8,128)(2,1)} %cotangent_ref.1, bf16[192,768]{1,0:T(8,128)(2,1)} %bitcast.14, bf16[192,768]{1,0:T(8,128)(2,1)} %bitcast.15, ...), custom_call_target="tpu_custom_call" | custom-call | tf_op jit(solution)/shard_map/attention/pallas_call | solution.py:116
  31.7 0.0 reduce-scatter.2.cloned.1.call-update
  31.8 33.2 %exchange_bias.1.bias_ref = f32[16,64,128]{2,1,0:T(8,128)} custom-call(bf16[4,512,512]{2,1,0:T(8,128)(2,1)} %get-tuple-element.10.part_ref), custom_call_target="tpu_custom_call" | custom-call | tf_op jit(solution)/shard_map/exchange_bias/pallas_call | solution.py:455
  65.0 36.3 %pair_transitions.1 = (bf16[128,64,128]{2,1,0:T(8,128)(2,1)}, bf16[768,256]{1,0:T(8,128)(2,1)}) custom-call(bf16[128,64,128]{2,1,0:T(8,128)(2,1)} %pair_ref.1, f32[16,64,128]{2,1,0:T(8,128)} %exchange_bias.1.bias_ref, bf16[16,128]{1,0:T(8,128)(2,1)} %bitcast.18, bf16[2,128,256]{2,1,0:T(8,128)(2,1)} %tg_ref.1, bf16[2,128,256]{2,1,0:T(8,128)(2,1)} %tu_ref.1, ...), custom_call_target="tpu_custom_call" | custom-call | tf_op jit(solution)/shard_map/pair_transitions/pallas_call | solution.py:210
  101.3 25.9 %sum_everywhere.1 = f32[8,96,256]{2,1,0:T(8,128)} custom-call(bf16[768,256]{1,0:T(8,128)(2,1)} %get-tuple-element.12.part_ref), custom_call_target="tpu_custom_call" | custom-call | tf_op jit(solution)/shard_map/sum_everywhere/pallas_call | solution.py:325
  127.2 2.0 %fusion.3 = (f32[1,2,128,256]{3,2,1,0:T(8,128)S(1)}, f32[2,128,256]{2,1,0:T(8,128)}, f32[2,128,256]{2,1,0:T(8,128)}) fusion(f32[3,2,128,256]{3,2,1,0:T(8,128)} %bitcast.13), kind=kLoop, calls=%fused_computation.12 | loop fusion | bytes 1572864 | tf_op jit(solution)/shard_map/slice | solution.py:509
  129.1 0.8 copy.19
  130.0 0.0 reduce-scatter.2.cloned.1.call-done
  (3 shorter events, 0.0 us)
Async XLA Ops:
  7.2 122.8 %reduce-scatter.2.cloned.1.call-start = ((), (), s32[]{:S(2)}) async-start(), calls=%async_computation.1 | async-start | bytes 1966080 | tf_op jit(solution)/shard_map/reduce_scatter | solution.py:497
Sparse Core Ops, SparseCore 0:
  31.9 42.1 reduce-scatter.1
